TPU v7x, 32 devices: a whole 2x2x4 slice. The times are simulated.
32 devices in a mesh: parts: 2 (over x), blk: 8 (over z, y), heads: 2 (over core).
Axes of the slice: x: 2, y: 2, z: 4, core: 2. Of those that a mesh axis runs over, the one named last changes fastest.
Arguments:
- frames: bfloat16 [12288, 1024], P(('parts', 'blk', 'heads')), parts along dimension 0, may hold values from -6 to 6
- modulation: float32 [6, 1024], P('parts'), parts along dimension 0, may hold values from -3 to 3
- w_qkv: bfloat16 [1024, 3072], replicated, may hold values from -4 to 4
- w_out: bfloat16 [1024, 1024], replicated, may hold values from -0.1875 to 0.1875
- turn_id: int32 [96], P('parts'), parts along dimension 0, may hold values from 0 to 11, never falling along the last dimension, each value on 1 to 12 neighbouring positions
- speaker: int32 [96], P('parts'), parts along dimension 0, may hold values from 0 to 3
- ref_flag: int32 [96], P('parts'), parts along dimension 0, may hold values from 0 to 1, as said below
Outputs:
- mixed: bfloat16 [12288, 1024], P(('parts', 'blk', 'heads')), parts along dimension 0
There are 2 independent parts, one for each index of `parts`. A program takes and returns all parts, laid end to end along the dimension named above; an argument that names none is the same for every part. Nothing has to cross between parts.
Inputs may be any that keep to these rules, and one draw needn't show every extreme that they name: `turn_id`: turn ids never fall along the sequence; each turn covers 1 to 12 consecutive blocks, one exactly 12. `ref_flag`: each aligned group of 6 blocks holds at most 2 reference blocks, some group exactly 2.
All inputs are finite; a program needn't handle non-finite values.
Results may differ from a plain program's by a relative error of at most 0.0034.
The roundings to bfloat16 on the way count: a program that leaves them out, or rounds other values in their place, can miss the bound.
Values may be sent and summed in bfloat16 or wider, within the bound.
A program may use at most 128 MiB of HBM per device.

v0:
```python
import math

import jax
import jax.numpy as jnp
from jax import lax
from jax.sharding import PartitionSpec as P

HEAD_DIM = 64
BLOCK = 128


norm_eps = 1e-06
neg_big = -1e30


def modulate(frames, modulation):
    widened = frames.astype(jnp.float32)
    average = jnp.mean(widened, axis=1, keepdims=True)
    centered = widened - average
    variance = jnp.mean(centered * centered, axis=1, keepdims=True)
    normed = centered * lax.rsqrt(variance + norm_eps)
    return (normed * (1.0 + modulation[1]) + modulation[0]).astype(jnp.bfloat16)


def lookup(table_row, positions):
    catalog = jnp.arange(table_row.shape[0], dtype=jnp.int32)
    picked = jnp.where(positions[:, None] == catalog[None, :], table_row[None, :], 0)
    return jnp.sum(picked, axis=1)


def attend_tile(state_now, queries, key_tile, allowed, score_scale):
    running_max, denominator, weighted = state_now
    row_count, local_heads, head_depth = queries.shape
    key_rows = key_tile[:, 0].reshape(-1, local_heads, head_depth)
    values = key_tile[:, 1].reshape(-1, local_heads, head_depth)
    scores = (
        jnp.einsum("qhd,khd->hqk", queries, key_rows, preferred_element_type=jnp.float32)
        * score_scale
    )
    scores = jnp.where(allowed[None], scores, neg_big)
    new_max = jnp.maximum(running_max, jnp.max(scores, axis=2))
    weights = jnp.where(allowed[None], jnp.exp(scores - new_max[:, :, None]), 0.0)
    factor = jnp.exp(running_max - new_max)
    denominator = denominator * factor + jnp.sum(weights, axis=2)
    weighted = weighted * factor.T[:, :, None] + jnp.einsum(
        "hqk,khd->qhd", weights.astype(jnp.bfloat16), values, preferred_element_type=jnp.float32
    )
    return (new_max, denominator, weighted)


def masked_tile(state_now, queries, key_tile, allowed, score_scale):
    return lax.cond(
        jnp.any(allowed),
        lambda inner_state: attend_tile(inner_state, queries, key_tile, allowed, score_scale),
        lambda inner_state: inner_state,
        state_now,
    )


def fold_keys(state_now, shard_piece, queries, mask_rule, score_scale):
    piece_rows = shard_piece.shape[0]
    tile_rows = math.gcd(piece_rows, queries.shape[0])
    stacked = shard_piece.reshape((piece_rows // tile_rows, tile_rows) + shard_piece.shape[1:])

    def tile_step(carried, tile_item):
        tile_index, key_tile = tile_item
        allowed = mask_rule(tile_index * tile_rows, tile_rows)
        return (masked_tile(carried, queries, key_tile, allowed, score_scale), None)

    result, _ = lax.scan(
        tile_step, state_now, (jnp.arange(piece_rows // tile_rows, dtype=jnp.int32), stacked)
    )
    return result


def per_device(frames, modulation, w_qkv, w_out, turn_id, speaker, ref_flag):
    head_groups = lax.axis_size("heads")
    blk_index = lax.axis_index("blk")
    local_rows, width_all = frames.shape
    modded = modulate(frames, modulation)
    projected = jnp.dot(modded, w_qkv, preferred_element_type=jnp.float32).astype(jnp.bfloat16)
    projected = projected.reshape(local_rows, 3, head_groups, width_all // head_groups)
    regrouped = lax.all_to_all(projected, "heads", split_axis=2, concat_axis=0, tiled=True)
    row_count = regrouped.shape[0]
    group_width = regrouped.shape[3]
    local_heads = group_width // HEAD_DIM
    queries = regrouped[:, 0, 0].reshape(row_count, local_heads, HEAD_DIM)
    kv_pairs = regrouped[:, 1:, 0]
    group_blocks = row_count // BLOCK
    query_blocks = blk_index * group_blocks + jnp.arange(row_count, dtype=jnp.int32) // BLOCK
    turn_q = lookup(turn_id, query_blocks)
    speak_q = lookup(speaker, query_blocks)
    score_scale = HEAD_DIM ** (-0.5)
    state_now = (
        jnp.full((local_heads, row_count), neg_big, jnp.float32),
        jnp.zeros((local_heads, row_count), jnp.float32),
        jnp.zeros((row_count, local_heads, HEAD_DIM), jnp.float32),
    )

    def rule_all(first_row, tile_rows):
        key_blocks = (first_row + jnp.arange(tile_rows, dtype=jnp.int32)) // BLOCK
        turn_k = lookup(turn_id, key_blocks)
        speak_k = lookup(speaker, key_blocks)
        ref_k = lookup(ref_flag, key_blocks)
        return (turn_q[:, None] == turn_k[None, :]) | (ref_k[None, :] == 1) & (
            speak_q[:, None] == speak_k[None, :]
        )

    state_now = fold_keys(
        state_now,
        lax.all_gather(kv_pairs, "blk", axis=0, tiled=True),
        queries,
        rule_all,
        score_scale,
    )
    running_max, denominator, weighted = state_now
    attended = (
        (weighted / denominator.T[:, :, None]).reshape(row_count, group_width).astype(jnp.bfloat16)
    )
    returned = lax.all_to_all(attended, "heads", split_axis=0, concat_axis=1, tiled=True)
    product = jnp.dot(returned, w_out, preferred_element_type=jnp.float32)
    return (frames.astype(jnp.float32) + modulation[2] * product).astype(jnp.bfloat16)


def solution(mesh):
    return jax.shard_map(
        per_device,
        mesh=mesh,
        in_specs=(
            P(("parts", "blk", "heads"), None),
            P("parts", None),
            P(),
            P(),
            P("parts"),
            P("parts"),
            P("parts"),
        ),
        out_specs=P(("parts", "blk", "heads"), None),
        check_vma=False,
    )
```

profile of v0, /device:TPU:15, one launch (start us, length us, event | category | flops | bytes accessed | tf_op | source)
XLA Modules:
  0.0 525.8 jit_solution(4009364159597707719)
XLA Ops:
  10.8 7.2 %convolution_convert_fusion = bf16[384,3072]{1,0:T(8,128)(2,1)} fusion(bf16[1024,3072]{1,0:T(8,128)(2,1)} %param.13, bf16[384,1024]{1,0:T(8,128)(2,1)} %param.11, f32[1024]{0:T(1024)S(1)} %bitcast.54, f32[1024]{0:T(1024)S(1)} %bitcast.55, f32[384]{0:T(512)S(1)} %add_rsqrt_fusion, f32[384]{0:T(512)S(1)} %broadcast_multiply_fusion), kind=kOutput, calls=%fused_computation.30 | convolution fusion | flops 2419458048 | bytes 9448448 | tf_op jit(solution)/shard_map/dot_general | solution.py:81
  39.9 169.9 %all-gather.3.cloned.1.call-done = bf16[6144,2,1,512]{3,0,1,2:T(8,128)(2,1)} async-done(((bf16[768,2,1,512]{3,0,1,2:T(8,128)(2,1)}), bf16[6144,2,1,512]{3,0,1,2:T(8,128)(2,1)}) %all-gather.3.cloned.1.call-update) | async-done | bytes 12582928 | tf_op jit(solution)/shard_map/all_gather | solution.py:111
  209.8 16.6 %copy.28 = bf16[8,768,2,512]{1,3,2,0:T(8,128)(2,1)} copy(bf16[8,768,2,512]{3,1,0,2:T(8,128)(2,1)} %bitcast.49) | data formatting | bytes 25165824 | tf_op jit(solution)/shard_map/while | solution.py:70
  228.8 276.7 %while.16 = (s32[]{:T(128)}, f32[8,768]{1,0:T(8,128)S(1)}, f32[8,768]{1,0:T(8,128)}, f32[768,8,64]{0,2,1:T(8,128)}, s32[768]{0:T(1024)S(1)}, /*index=5*/s32[8]{0...) while((s32[]{:T(128)}, f32[8,768]{1,0:T(8,128)S(1)}, ...), condition=%wide.region_13.14_spmd, body=%wide.region_4.13_spmd.sunk | while | flops 1273324032 | bytes 71205208 | solution.py:70
  238.7 33.9 %conditional.2 = ((f32[8,768]{1,0:T(8,128)S(1)}, f32[8,768]{1,0:T(8,128)}, f32[768,8,64]{0,2,1:T(8,128)})) conditional(s32[]{:T(128)} %convert_element_type.64, (f32[8,768]{1,0:T(8,128)S(1)}, f32[8,768]{1,0:T(8,128)}, f32[768,8,64]{0,2,1:T(8,128)}) %tuple.54, (pred[768,768]{0,1:T(8,128)(4,1)S(1)}, bf16[8,768,2,512]{1,3,2,0:T(8,128)(2,1)}, ...), branch_computations={%region_9.9_spmd, %region_10.12_spmd} | conditional | flops 1270106112 | bytes 70582304 | solution.py:52
  241.2 8.1 %fusion = (f32[8,768]{1,0:T(8,128)S(1)}, f32[8,768,768]{2,1,0:T(8,128)}) fusion(pred[768,768]{0,1:T(8,128)(4,1)S(1)} %get-tuple-element.185, bf16[768,8,64]{0,2,1:T(8,128)(2,1)S(1)} %bitcast.46, bf16[768,8,64]{0,2,1:T(8,128)(2,1)S(1)} %get-tuple-element.188), kind=kOutput, calls=%fused_computation.2 | convolution fusion | flops 618129408 | bytes 21061632 | tf_op jit(solution)/shard_map/while/body/eval_jaxpr/cond/branch_1_fun/qhd,khd->hqk/dot_general | solution.py:37
  249.9 10.8 %fusion.2 = f32[8,768]{1,0:T(8,128)S(1)} fusion(f32[8,768,768]{2,1,0:T(8,128)} %get-tuple-element.295, f32[8,768]{1,0:T(8,128)S(1)} %get-tuple-element.391, pred[768,768]{0,1:T(8,128)(4,1)S(1)} %get-tuple-element.185), kind=kLoop, calls=%fused_computation.4 | loop fusion | flops 23586816 | bytes 19513344 | tf_op jit(solution)/shard_map/while/body/eval_jaxpr/cond/branch_1_fun/reduce_sum | solution.py:44
  262.1 10.5 %bitcast_add_fusion = f32[768,8,64]{0,2,1:T(8,128)} fusion(f32[768,8,64]{0,2,1:T(8,128)} %get-tuple-element.190, bf16[768,8,64]{0,2,1:T(8,128)(2,1)} %bitcast.48, f32[8,768,768]{2,1,0:T(8,128)} %get-tuple-element.295, f32[8,768]{1,0:T(8,128)S(1)} %get-tuple-element.391, pred[768,768]{0,1:T(8,128)(4,1)S(1)} %get-tuple-element.185, ...), kind=kOutput, calls=%fused_computation.7 | convolution fusion | flops 628359168 | bytes 23445504 | tf_op jit(solution)/shard_map/while/body/eval_jaxpr/cond/branch_1_fun/hqk,khd->qhd/dot_general | solution.py:45
  277.5 33.9 %conditional.2 = ((f32[8,768]{1,0:T(8,128)S(1)}, f32[8,768]{1,0:T(8,128)}, f32[768,8,64]{0,2,1:T(8,128)})) conditional(s32[]{:T(128)} %convert_element_type.64, (f32[8,768]{1,0:T(8,128)S(1)}, f32[8,768]{1,0:T(8,128)}, f32[768,8,64]{0,2,1:T(8,128)}) %tuple.54, (pred[768,768]{0,1:T(8,128)(4,1)S(1)}, bf16[8,768,2,512]{1,3,2,0:T(8,128)(2,1)}, ...), branch_computations={%region_9.9_spmd, %region_10.12_spmd} | conditional | flops 1270106112 | bytes 70582304 | solution.py:52
  280.0 8.1 %fusion = (f32[8,768]{1,0:T(8,128)S(1)}, f32[8,768,768]{2,1,0:T(8,128)}) fusion(pred[768,768]{0,1:T(8,128)(4,1)S(1)} %get-tuple-element.185, bf16[768,8,64]{0,2,1:T(8,128)(2,1)S(1)} %bitcast.46, bf16[768,8,64]{0,2,1:T(8,128)(2,1)S(1)} %get-tuple-element.188), kind=kOutput, calls=%fused_computation.2 | convolution fusion | flops 618129408 | bytes 21061632 | tf_op jit(solution)/shard_map/while/body/eval_jaxpr/cond/branch_1_fun/qhd,khd->hqk/dot_general | solution.py:37
  288.7 10.8 %fusion.2 = f32[8,768]{1,0:T(8,128)S(1)} fusion(f32[8,768,768]{2,1,0:T(8,128)} %get-tuple-element.295, f32[8,768]{1,0:T(8,128)S(1)} %get-tuple-element.391, pred[768,768]{0,1:T(8,128)(4,1)S(1)} %get-tuple-element.185), kind=kLoop, calls=%fused_computation.4 | loop fusion | flops 23586816 | bytes 19513344 | tf_op jit(solution)/shard_map/while/body/eval_jaxpr/cond/branch_1_fun/reduce_sum | solution.py:44
  300.9 10.5 %bitcast_add_fusion = f32[768,8,64]{0,2,1:T(8,128)} fusion(f32[768,8,64]{0,2,1:T(8,128)} %get-tuple-element.190, bf16[768,8,64]{0,2,1:T(8,128)(2,1)} %bitcast.48, f32[8,768,768]{2,1,0:T(8,128)} %get-tuple-element.295, f32[8,768]{1,0:T(8,128)S(1)} %get-tuple-element.391, pred[768,768]{0,1:T(8,128)(4,1)S(1)} %get-tuple-element.185, ...), kind=kOutput, calls=%fused_computation.7 | convolution fusion | flops 628359168 | bytes 23445504 | tf_op jit(solution)/shard_map/while/body/eval_jaxpr/cond/branch_1_fun/hqk,khd->qhd/dot_general | solution.py:45
  316.3 33.9 %conditional.2 = ((f32[8,768]{1,0:T(8,128)S(1)}, f32[8,768]{1,0:T(8,128)}, f32[768,8,64]{0,2,1:T(8,128)})) conditional(s32[]{:T(128)} %convert_element_type.64, (f32[8,768]{1,0:T(8,128)S(1)}, f32[8,768]{1,0:T(8,128)}, f32[768,8,64]{0,2,1:T(8,128)}) %tuple.54, (pred[768,768]{0,1:T(8,128)(4,1)S(1)}, bf16[8,768,2,512]{1,3,2,0:T(8,128)(2,1)}, ...), branch_computations={%region_9.9_spmd, %region_10.12_spmd} | conditional | flops 1270106112 | bytes 70582304 | solution.py:52
  318.8 8.1 %fusion = (f32[8,768]{1,0:T(8,128)S(1)}, f32[8,768,768]{2,1,0:T(8,128)}) fusion(pred[768,768]{0,1:T(8,128)(4,1)S(1)} %get-tuple-element.185, bf16[768,8,64]{0,2,1:T(8,128)(2,1)S(1)} %bitcast.46, bf16[768,8,64]{0,2,1:T(8,128)(2,1)S(1)} %get-tuple-element.188), kind=kOutput, calls=%fused_computation.2 | convolution fusion | flops 618129408 | bytes 21061632 | tf_op jit(solution)/shard_map/while/body/eval_jaxpr/cond/branch_1_fun/qhd,khd->hqk/dot_general | solution.py:37
  327.5 10.8 %fusion.2 = f32[8,768]{1,0:T(8,128)S(1)} fusion(f32[8,768,768]{2,1,0:T(8,128)} %get-tuple-element.295, f32[8,768]{1,0:T(8,128)S(1)} %get-tuple-element.391, pred[768,768]{0,1:T(8,128)(4,1)S(1)} %get-tuple-element.185), kind=kLoop, calls=%fused_computation.4 | loop fusion | flops 23586816 | bytes 19513344 | tf_op jit(solution)/shard_map/while/body/eval_jaxpr/cond/branch_1_fun/reduce_sum | solution.py:44
  339.7 10.5 %bitcast_add_fusion = f32[768,8,64]{0,2,1:T(8,128)} fusion(f32[768,8,64]{0,2,1:T(8,128)} %get-tuple-element.190, bf16[768,8,64]{0,2,1:T(8,128)(2,1)} %bitcast.48, f32[8,768,768]{2,1,0:T(8,128)} %get-tuple-element.295, f32[8,768]{1,0:T(8,128)S(1)} %get-tuple-element.391, pred[768,768]{0,1:T(8,128)(4,1)S(1)} %get-tuple-element.185, ...), kind=kOutput, calls=%fused_computation.7 | convolution fusion | flops 628359168 | bytes 23445504 | tf_op jit(solution)/shard_map/while/body/eval_jaxpr/cond/branch_1_fun/hqk,khd->qhd/dot_general | solution.py:45
  355.1 33.9 %conditional.2 = ((f32[8,768]{1,0:T(8,128)S(1)}, f32[8,768]{1,0:T(8,128)}, f32[768,8,64]{0,2,1:T(8,128)})) conditional(s32[]{:T(128)} %convert_element_type.64, (f32[8,768]{1,0:T(8,128)S(1)}, f32[8,768]{1,0:T(8,128)}, f32[768,8,64]{0,2,1:T(8,128)}) %tuple.54, (pred[768,768]{0,1:T(8,128)(4,1)S(1)}, bf16[8,768,2,512]{1,3,2,0:T(8,128)(2,1)}, ...), branch_computations={%region_9.9_spmd, %region_10.12_spmd} | conditional | flops 1270106112 | bytes 70582304 | solution.py:52
  357.7 8.1 %fusion = (f32[8,768]{1,0:T(8,128)S(1)}, f32[8,768,768]{2,1,0:T(8,128)}) fusion(pred[768,768]{0,1:T(8,128)(4,1)S(1)} %get-tuple-element.185, bf16[768,8,64]{0,2,1:T(8,128)(2,1)S(1)} %bitcast.46, bf16[768,8,64]{0,2,1:T(8,128)(2,1)S(1)} %get-tuple-element.188), kind=kOutput, calls=%fused_computation.2 | convolution fusion | flops 618129408 | bytes 21061632 | tf_op jit(solution)/shard_map/while/body/eval_jaxpr/cond/branch_1_fun/qhd,khd->hqk/dot_general | solution.py:37
  366.4 10.8 %fusion.2 = f32[8,768]{1,0:T(8,128)S(1)} fusion(f32[8,768,768]{2,1,0:T(8,128)} %get-tuple-element.295, f32[8,768]{1,0:T(8,128)S(1)} %get-tuple-element.391, pred[768,768]{0,1:T(8,128)(4,1)S(1)} %get-tuple-element.185), kind=kLoop, calls=%fused_computation.4 | loop fusion | flops 23586816 | bytes 19513344 | tf_op jit(solution)/shard_map/while/body/eval_jaxpr/cond/branch_1_fun/reduce_sum | solution.py:44
  378.5 10.5 %bitcast_add_fusion = f32[768,8,64]{0,2,1:T(8,128)} fusion(f32[768,8,64]{0,2,1:T(8,128)} %get-tuple-element.190, bf16[768,8,64]{0,2,1:T(8,128)(2,1)} %bitcast.48, f32[8,768,768]{2,1,0:T(8,128)} %get-tuple-element.295, f32[8,768]{1,0:T(8,128)S(1)} %get-tuple-element.391, pred[768,768]{0,1:T(8,128)(4,1)S(1)} %get-tuple-element.185, ...), kind=kOutput, calls=%fused_computation.7 | convolution fusion | flops 628359168 | bytes 23445504 | tf_op jit(solution)/shard_map/while/body/eval_jaxpr/cond/branch_1_fun/hqk,khd->qhd/dot_general | solution.py:45
  394.0 33.9 %conditional.2 = ((f32[8,768]{1,0:T(8,128)S(1)}, f32[8,768]{1,0:T(8,128)}, f32[768,8,64]{0,2,1:T(8,128)})) conditional(s32[]{:T(128)} %convert_element_type.64, (f32[8,768]{1,0:T(8,128)S(1)}, f32[8,768]{1,0:T(8,128)}, f32[768,8,64]{0,2,1:T(8,128)}) %tuple.54, (pred[768,768]{0,1:T(8,128)(4,1)S(1)}, bf16[8,768,2,512]{1,3,2,0:T(8,128)(2,1)}, ...), branch_computations={%region_9.9_spmd, %region_10.12_spmd} | conditional | flops 1270106112 | bytes 70582304 | solution.py:52
  396.5 8.1 %fusion = (f32[8,768]{1,0:T(8,128)S(1)}, f32[8,768,768]{2,1,0:T(8,128)}) fusion(pred[768,768]{0,1:T(8,128)(4,1)S(1)} %get-tuple-element.185, bf16[768,8,64]{0,2,1:T(8,128)(2,1)S(1)} %bitcast.46, bf16[768,8,64]{0,2,1:T(8,128)(2,1)S(1)} %get-tuple-element.188), kind=kOutput, calls=%fused_computation.2 | convolution fusion | flops 618129408 | bytes 21061632 | tf_op jit(solution)/shard_map/while/body/eval_jaxpr/cond/branch_1_fun/qhd,khd->hqk/dot_general | solution.py:37
  405.2 10.8 %fusion.2 = f32[8,768]{1,0:T(8,128)S(1)} fusion(f32[8,768,768]{2,1,0:T(8,128)} %get-tuple-element.295, f32[8,768]{1,0:T(8,128)S(1)} %get-tuple-element.391, pred[768,768]{0,1:T(8,128)(4,1)S(1)} %get-tuple-element.185), kind=kLoop, calls=%fused_computation.4 | loop fusion | flops 23586816 | bytes 19513344 | tf_op jit(solution)/shard_map/while/body/eval_jaxpr/cond/branch_1_fun/reduce_sum | solution.py:44
  417.4 10.5 %bitcast_add_fusion = f32[768,8,64]{0,2,1:T(8,128)} fusion(f32[768,8,64]{0,2,1:T(8,128)} %get-tuple-element.190, bf16[768,8,64]{0,2,1:T(8,128)(2,1)} %bitcast.48, f32[8,768,768]{2,1,0:T(8,128)} %get-tuple-element.295, f32[8,768]{1,0:T(8,128)S(1)} %get-tuple-element.391, pred[768,768]{0,1:T(8,128)(4,1)S(1)} %get-tuple-element.185, ...), kind=kOutput, calls=%fused_computation.7 | convolution fusion | flops 628359168 | bytes 23445504 | tf_op jit(solution)/shard_map/while/body/eval_jaxpr/cond/branch_1_fun/hqk,khd->qhd/dot_general | solution.py:45
  432.8 33.9 %conditional.2 = ((f32[8,768]{1,0:T(8,128)S(1)}, f32[8,768]{1,0:T(8,128)}, f32[768,8,64]{0,2,1:T(8,128)})) conditional(s32[]{:T(128)} %convert_element_type.64, (f32[8,768]{1,0:T(8,128)S(1)}, f32[8,768]{1,0:T(8,128)}, f32[768,8,64]{0,2,1:T(8,128)}) %tuple.54, (pred[768,768]{0,1:T(8,128)(4,1)S(1)}, bf16[8,768,2,512]{1,3,2,0:T(8,128)(2,1)}, ...), branch_computations={%region_9.9_spmd, %region_10.12_spmd} | conditional | flops 1270106112 | bytes 70582304 | solution.py:52
  435.3 8.1 %fusion = (f32[8,768]{1,0:T(8,128)S(1)}, f32[8,768,768]{2,1,0:T(8,128)}) fusion(pred[768,768]{0,1:T(8,128)(4,1)S(1)} %get-tuple-element.185, bf16[768,8,64]{0,2,1:T(8,128)(2,1)S(1)} %bitcast.46, bf16[768,8,64]{0,2,1:T(8,128)(2,1)S(1)} %get-tuple-element.188), kind=kOutput, calls=%fused_computation.2 | convolution fusion | flops 618129408 | bytes 21061632 | tf_op jit(solution)/shard_map/while/body/eval_jaxpr/cond/branch_1_fun/qhd,khd->hqk/dot_general | solution.py:37
  444.0 10.8 %fusion.2 = f32[8,768]{1,0:T(8,128)S(1)} fusion(f32[8,768,768]{2,1,0:T(8,128)} %get-tuple-element.295, f32[8,768]{1,0:T(8,128)S(1)} %get-tuple-element.391, pred[768,768]{0,1:T(8,128)(4,1)S(1)} %get-tuple-element.185), kind=kLoop, calls=%fused_computation.4 | loop fusion | flops 23586816 | bytes 19513344 | tf_op jit(solution)/shard_map/while/body/eval_jaxpr/cond/branch_1_fun/reduce_sum | solution.py:44
  456.2 10.5 %bitcast_add_fusion = f32[768,8,64]{0,2,1:T(8,128)} fusion(f32[768,8,64]{0,2,1:T(8,128)} %get-tuple-element.190, bf16[768,8,64]{0,2,1:T(8,128)(2,1)} %bitcast.48, f32[8,768,768]{2,1,0:T(8,128)} %get-tuple-element.295, f32[8,768]{1,0:T(8,128)S(1)} %get-tuple-element.391, pred[768,768]{0,1:T(8,128)(4,1)S(1)} %get-tuple-element.185, ...), kind=kOutput, calls=%fused_computation.7 | convolution fusion | flops 628359168 | bytes 23445504 | tf_op jit(solution)/shard_map/while/body/eval_jaxpr/cond/branch_1_fun/hqk,khd->qhd/dot_general | solution.py:45
  471.6 33.9 %conditional.2 = ((f32[8,768]{1,0:T(8,128)S(1)}, f32[8,768]{1,0:T(8,128)}, f32[768,8,64]{0,2,1:T(8,128)})) conditional(s32[]{:T(128)} %convert_element_type.64, (f32[8,768]{1,0:T(8,128)S(1)}, f32[8,768]{1,0:T(8,128)}, f32[768,8,64]{0,2,1:T(8,128)}) %tuple.54, (pred[768,768]{0,1:T(8,128)(4,1)S(1)}, bf16[8,768,2,512]{1,3,2,0:T(8,128)(2,1)}, ...), branch_computations={%region_9.9_spmd, %region_10.12_spmd} | conditional | flops 1270106112 | bytes 70582304 | solution.py:52
  474.1 8.1 %fusion = (f32[8,768]{1,0:T(8,128)S(1)}, f32[8,768,768]{2,1,0:T(8,128)}) fusion(pred[768,768]{0,1:T(8,128)(4,1)S(1)} %get-tuple-element.185, bf16[768,8,64]{0,2,1:T(8,128)(2,1)S(1)} %bitcast.46, bf16[768,8,64]{0,2,1:T(8,128)(2,1)S(1)} %get-tuple-element.188), kind=kOutput, calls=%fused_computation.2 | convolution fusion | flops 618129408 | bytes 21061632 | tf_op jit(solution)/shard_map/while/body/eval_jaxpr/cond/branch_1_fun/qhd,khd->hqk/dot_general | solution.py:37
  482.8 10.8 %fusion.2 = f32[8,768]{1,0:T(8,128)S(1)} fusion(f32[8,768,768]{2,1,0:T(8,128)} %get-tuple-element.295, f32[8,768]{1,0:T(8,128)S(1)} %get-tuple-element.391, pred[768,768]{0,1:T(8,128)(4,1)S(1)} %get-tuple-element.185), kind=kLoop, calls=%fused_computation.4 | loop fusion | flops 23586816 | bytes 19513344 | tf_op jit(solution)/shard_map/while/body/eval_jaxpr/cond/branch_1_fun/reduce_sum | solution.py:44
  495.0 10.5 %bitcast_add_fusion = f32[768,8,64]{0,2,1:T(8,128)} fusion(f32[768,8,64]{0,2,1:T(8,128)} %get-tuple-element.190, bf16[768,8,64]{0,2,1:T(8,128)(2,1)} %bitcast.48, f32[8,768,768]{2,1,0:T(8,128)} %get-tuple-element.295, f32[8,768]{1,0:T(8,128)S(1)} %get-tuple-element.391, pred[768,768]{0,1:T(8,128)(4,1)S(1)} %get-tuple-element.185, ...), kind=kOutput, calls=%fused_computation.7 | convolution fusion | flops 628359168 | bytes 23445504 | tf_op jit(solution)/shard_map/while/body/eval_jaxpr/cond/branch_1_fun/hqk,khd->qhd/dot_general | solution.py:45
  (109 shorter events, 101.8 us)
Async XLA Ops:
  6.5 510.5 %copy-start = (bf16[1024,1024]{1,0:T(8,128)(2,1)S(1)}, bf16[1024,1024]{1,0:T(8,128)(2,1)}, u32[]{:S(2)}) copy-start(bf16[1024,1024]{1,0:T(8,128)(2,1)} %param.14) | copy-start | bytes 6291460
  6.5 203.2 %all-gather.3.cloned.1.call-start = ((), (), s32[]{:S(2)}) async-start(), calls=%async_computation.2 | async-start | bytes 14155776 | tf_op jit(solution)/shard_map/all_gather | solution.py:111
  32.9 1.4 copy-start.1
  507.9 9.1 %copy-start.2 = (bf16[384,1024]{1,0:T(8,128)(2,1)S(1)}, bf16[384,1024]{1,0:T(8,128)(2,1)}, u32[]{:S(2)}) copy-start(bf16[384,1024]{1,0:T(8,128)(2,1)} %param.11) | copy-start | bytes 2359300
  507.9 9.1 %copy-start.3 = (f32[1,1024]{1,0:T(1,128)S(1)}, f32[1,1024]{1,0:T(1,128)}, u32[]{:S(2)}) copy-start(f32[1,1024]{1,0:T(1,128)} %get-tuple-element.296) | copy-start | bytes 12292
Sparse Core Ops, SparseCore 0:
  35.7 173.9 all-gather.2
where the time goes:
time: 529 us; the launch traced here: 526 us
  waiting for transfers between devices  170 us (32%)
  matrix products  139 us (26%)
  other arithmetic  116 us (22%)
  local copies, waits for them, and re-layouts  65.2 us (12%)
  between operations  13.5 us (3%)
  blocking collectives  11.1 us (2%)
  loops' own time  10.8 us (2%)
    all_gather x1, waiting for transfers between devices, per_device(): lax.all_gather(kv_pairs, 'blk', axis=0, tiled=True)  170 us
    reduce_sum x7, other arithmetic, attend_tile(): denominator = denominator * factor + jnp.sum(weights, axis=2)  75.7 us
    dot_general x7, matrix products, attend_tile(): jnp.einsum('hqk,khd->qhd', weights.astype(jnp.bfloat16), values, preferre...  73.6 us
    dot_general x7, matrix products, attend_tile(): jnp.einsum('qhd,khd->hqk', queries, key_rows, preferred_element_type=jnp....  56.6 us
    while x1, local copies, waits for them, and re-layouts, fold_keys(): lax.scan(tile_step, state_now, (jnp.arange(piece_rows // tile_rows, dtype...  16.6 us
    reduce_or x8, other arithmetic, masked_tile(): jnp.any(allowed)  12.5 us
    another operation x1, loops' own time, fold_keys(): lax.scan(tile_step, state_now, (jnp.arange(piece_rows // tile_rows, dtype...  10.6 us
    squeeze x7, local copies, waits for them, and re-layouts, fold_keys(): lax.scan(tile_step, state_now, (jnp.arange(piece_rows // tile_rows, dtype...  10.6 us
  transfers between devices with their start and end apart: 1, of which 1 were waited for; matrix products, arithmetic and copies ran while one was open for 1% of the time, Pallas kernels for 0%

commit v1 on v0

v1 whole, which is shorter than its diff:
```python
import jax
import jax.numpy as jnp
from jax import lax
from jax.experimental import pallas as pl
from jax.experimental.pallas import tpu as pltpu
from jax.sharding import PartitionSpec as P

HEAD_DIM = 64
BLOCK = 128
TURN_MAX = 12
REF_DEV = 2
CHUNK = 4

norm_eps = 1e-06
score_factor = HEAD_DIM ** (-0.5) * 1.4426950408889634


def modulate(frames, modulation):
    widened = frames.astype(jnp.float32)
    average = jnp.mean(widened, axis=1, keepdims=True)
    centered = widened - average
    variance = jnp.mean(centered * centered, axis=1, keepdims=True)
    normed = centered * lax.rsqrt(variance + norm_eps)
    return (normed * (1.0 + modulation[1]) + modulation[0]).astype(jnp.bfloat16)


def attend_kernel(
    turn, speaker, ref_flag, own, gathered, w_qkv, w_out, frames, modulation, out,
    need, lists, counts, kv, held, queries, top, total, weighted, attended, sems,
):
    blocks = turn.shape[0]
    width = own.shape[1]
    own_blocks = own.shape[0] // BLOCK
    pairs = width // (2 * HEAD_DIM)
    list_len = lists.shape[0] // own_blocks
    device = lax.axis_index("blk") * lax.axis_size("heads") + lax.axis_index("heads")
    first = device * own_blocks

    def scan_block(b, filled):
        slot, lengths = filled[0], filled[1:]
        used = jnp.int32(0)
        updated = []
        for i in range(own_blocks):
            fits = (turn[b] == turn[first + i]) | (
                (ref_flag[b] == 1) & (speaker[b] == speaker[first + i])
            )
            hit = jnp.where(fits, 1, 0).astype(jnp.int32)
            lists[i * list_len + lengths[i]] = slot
            updated.append(lengths[i] + hit)
            used = used | hit
        need[slot] = b
        return (slot + used, *updated)

    zero = jnp.int32(0)
    filled = lax.fori_loop(0, blocks, scan_block, (zero,) * (own_blocks + 1))
    needed = filled[0]
    for i in range(own_blocks):
        length = filled[1 + i]
        counts[i] = length
        lists[i * list_len + length] = lists[i * list_len + length - 1]
    for extra in range(CHUNK):
        need[needed + extra] = need[needed - 1]
    chunks = (needed + CHUNK - 1) // CHUNK

    def fetch(chunk, side):
        return [
            pltpu.make_async_copy(
                gathered.at[pl.ds(pl.multiple_of(need[chunk * CHUNK + k] * BLOCK, BLOCK), BLOCK)],
                held.at[side, pl.ds(k * BLOCK, BLOCK)],
                sems.at[side, k],
            )
            for k in range(CHUNK)
        ]

    for copy in fetch(0, 0):
        copy.start()

    lane = lax.broadcasted_iota(jnp.int32, (BLOCK, 2 * HEAD_DIM), 1)
    lower = lane < HEAD_DIM
    step = 512
    for col in range(0, width, step):
        part = jnp.dot(
            own[...], w_qkv[:, col : col + step], preferred_element_type=jnp.float32
        ).astype(jnp.bfloat16)
        for i in range(own_blocks):
            for local in range(step // (2 * HEAD_DIM)):
                tile = part[i * BLOCK : (i + 1) * BLOCK, local * 128 : (local + 1) * 128]
                p = col // (2 * HEAD_DIM) + local
                queries[i, p, :BLOCK] = jnp.where(lower, tile, 0).astype(jnp.bfloat16)
                queries[i, p, BLOCK:] = jnp.where(lower, 0, tile).astype(jnp.bfloat16)

    def project(chunk, _):
        side = lax.rem(chunk, 2)

        @pl.when(chunk + 1 < chunks)
        def _():
            for copy in fetch(chunk + 1, 1 - side):
                copy.start()

        for copy in fetch(chunk, side):
            copy.wait()
        rows = held[side]
        for col in range(0, 2 * width, step):
            part = jnp.dot(
                rows, w_qkv[:, width + col : width + col + step],
                preferred_element_type=jnp.float32,
            ).astype(jnp.bfloat16)
            kv[pl.ds(pl.multiple_of(chunk * CHUNK * BLOCK, BLOCK), CHUNK * BLOCK), col : col + step] = part
        return 0

    lax.fori_loop(0, chunks, project, 0)

    def one_query_block(i, _):
        length = counts[i]
        steps = (length + 1) // 2

        def rows_of(t):
            start = lists[i * list_len + t]
            return pl.ds(pl.multiple_of(start * BLOCK, BLOCK), BLOCK)

        def score(p, a, b):
            keys = jnp.concatenate(
                [kv[a, p * 128 : (p + 1) * 128], kv[b, p * 128 : (p + 1) * 128]], axis=0
            )
            return lax.dot_general(
                queries[i, p], keys, (((1,), (1,)), ((), ())), preferred_element_type=jnp.float32
            )

        top[...] = jnp.full(top.shape, -jnp.inf, jnp.float32)

        def find_top(t, _):
            a, b = rows_of(2 * t), rows_of(2 * t + 1)
            for p in range(pairs):
                s = score(p, a, b)
                top[p] = jnp.maximum(top[p], jnp.maximum(s[:, :BLOCK], s[:, BLOCK:]))
            return 0

        lax.fori_loop(0, steps, find_top, 0)
        for p in range(pairs):
            top[p] = jnp.broadcast_to(jnp.max(top[p], axis=1, keepdims=True), top.shape[1:])
        total[...] = jnp.zeros(total.shape, jnp.float32)
        weighted[...] = jnp.zeros(weighted.shape, jnp.float32)

        def add_up(t, _):
            a, b = rows_of(2 * t), rows_of(2 * t + 1)
            drop = jnp.where(2 * t + 1 < length, 0.0, 1e30).astype(jnp.float32)
            for p in range(pairs):
                s = score(p, a, b)
                high = top[p]
                wa = jnp.exp2((s[:, :BLOCK] - high) * score_factor)
                wb = jnp.exp2((s[:, BLOCK:] - (high + drop)) * score_factor)
                total[p] += wa + wb
                values = jnp.concatenate(
                    [
                        kv[a, width + p * 128 : width + (p + 1) * 128],
                        kv[b, width + p * 128 : width + (p + 1) * 128],
                    ],
                    axis=0,
                )
                weights = jnp.concatenate(
                    [wa.astype(jnp.bfloat16), wb.astype(jnp.bfloat16)], axis=1
                )
                weighted[p] += jnp.dot(weights, values, preferred_element_type=jnp.float32)
            return 0

        lax.fori_loop(0, steps, add_up, 0)
        at = pl.ds(pl.multiple_of(i * BLOCK, BLOCK), BLOCK)
        for p in range(pairs):
            ratio = weighted[p] / jnp.sum(total[p], axis=1, keepdims=True)
            attended[at, p * 128 : (p + 1) * 128] = jnp.where(
                lower, ratio[:BLOCK], ratio[BLOCK:]
            ).astype(jnp.bfloat16)
        return 0

    lax.fori_loop(0, own_blocks, one_query_block, 0)

    for col in range(0, width, step):
        product = jnp.dot(
            attended[...], w_out[:, col : col + step], preferred_element_type=jnp.float32
        )
        out[:, col : col + step] = (
            frames[:, col : col + step].astype(jnp.float32)
            + modulation[2:3, col : col + step] * product
        ).astype(jnp.bfloat16)


def attend(own, gathered, w_qkv, w_out, frames, modulation, turn_id, speaker, ref_flag):
    rows, width = frames.shape
    blocks = turn_id.shape[0]
    own_blocks = rows // BLOCK
    groups = lax.axis_size("blk")
    most = min(blocks, own_blocks + 2 * (TURN_MAX - 1) + REF_DEV * groups)
    slots = -(-most // CHUNK) * CHUNK
    list_len = min(blocks, TURN_MAX + REF_DEV * groups) + 4
    pairs = width // (2 * HEAD_DIM)
    smem = pl.BlockSpec(memory_space=pltpu.SMEM)
    vmem = pl.BlockSpec(memory_space=pltpu.VMEM)
    return pl.pallas_call(
        attend_kernel,
        out_shape=jax.ShapeDtypeStruct(frames.shape, jnp.bfloat16),
        in_specs=[smem] * 3 + [vmem, pl.BlockSpec(memory_space=pl.ANY)] + [vmem] * 4,
        out_specs=vmem,
        scratch_shapes=[
            pltpu.SMEM((slots + CHUNK + 4,), jnp.int32),
            pltpu.SMEM((own_blocks * list_len,), jnp.int32),
            pltpu.SMEM((own_blocks,), jnp.int32),
            pltpu.VMEM((slots * BLOCK, 2 * width), jnp.bfloat16),
            pltpu.VMEM((2, CHUNK * BLOCK, width), jnp.bfloat16),
            pltpu.VMEM((own_blocks, pairs, 2 * BLOCK, 2 * HEAD_DIM), jnp.bfloat16),
            pltpu.VMEM((pairs, 2 * BLOCK, BLOCK), jnp.float32),
            pltpu.VMEM((pairs, 2 * BLOCK, BLOCK), jnp.float32),
            pltpu.VMEM((pairs, 2 * BLOCK, 2 * HEAD_DIM), jnp.float32),
            pltpu.VMEM((rows, width), jnp.bfloat16),
            pltpu.SemaphoreType.DMA((2, CHUNK)),
        ],
        compiler_params=pltpu.CompilerParams(vmem_limit_bytes=62 * 1024 * 1024),
        cost_estimate=pl.CostEstimate(
            flops=20_000_000_000, bytes_accessed=20_000_000, transcendentals=10_000_000
        ),
    )(turn_id, speaker, ref_flag, own, gathered, w_qkv, w_out, frames, modulation)


def per_device(frames, modulation, w_qkv, w_out, turn_id, speaker, ref_flag):
    modded = modulate(frames, modulation)
    gathered = lax.all_gather(modded, ("blk", "heads"), axis=0, tiled=True)
    return attend(modded, gathered, w_qkv, w_out, frames, modulation, turn_id, speaker, ref_flag)


def solution(mesh):
    return jax.shard_map(
        per_device,
        mesh=mesh,
        in_specs=(
            P(("parts", "blk", "heads"), None),
            P("parts", None),
            P(),
            P(),
            P("parts"),
            P("parts"),
            P("parts"),
        ),
        out_specs=P(("parts", "blk", "heads"), None),
        check_vma=False,
    )
```

time: 529 us -> 172 us (0.33)
  the two profiles are of different devices: /device:TPU:15 before, /device:TPU:17 now
where the time goes in v1:
time: 172 us
  waiting for transfers between devices  102 us (59%)
  Pallas kernels  52.6 us (31%)
  between operations  13.4 us (8%)
  other arithmetic  4.18 us (2%)
    all_gather x1, waiting for transfers between devices, per_device(): gathered = lax.all_gather(modded, ('blk', 'heads'), axis=0, tiled=True)  102 us
    pallas_call x1, Pallas kernels, attend(): pl.pallas_call(attend_kernel, out_shape=jax.ShapeDtypeStruct(frames.shape...  52.6 us
  transfers between devices with their start and end apart: 1, of which 1 were waited for; matrix products, arithmetic and copies ran while one was open for 0% of the time, Pallas kernels for 0%

profile of v1, /device:TPU:17, one launch (start us, length us, event | category | flops | bytes accessed | tf_op | source)
XLA Modules:
  0.0 171.7 jit_solution(270904468848318621)
XLA Ops:
  6.5 0.0 copy-start
  6.5 0.0 copy-start.1
  6.5 0.0 all-gather.2.cloned.1.call-start
  6.5 1.4 convert_reduce_fusion
  7.9 1.5 fusion.2
  9.4 0.0 copy-done.1
  9.5 0.0 copy-done
  9.5 1.3 fusion.5.own
  10.8 0.0 all-gather.2.cloned.1.call-update
  10.8 101.5 %all-gather.2.cloned.1.call-done.gathered = bf16[6144,1024]{1,0:T(8,128)(2,1)} async-done(((bf16[384,1024]{1,0:T(8,128)(2,1)}), bf16[6144,1024]{1,0:T(8,128)(2,1)}) %all-gather.2.cloned.1.call-update) | async-done | bytes 12582928 | tf_op jit(solution)/shard_map/all_gather | solution.py:225
  112.3 52.6 %shard_map.73 = bf16[384,1024]{1,0:T(8,128)(2,1)} custom-call(s32[48]{0:T(128)} %turn.1, s32[48]{0:T(128)} %speaker.1, s32[48]{0:T(128)} %ref_flag.1, bf16[384,1024]{1,0:T(8,128)(2,1)} %fusion.5.own, bf16[6144,1024]{1,0:T(8,128)(2,1)} %all-gather.2.cloned.1.call-done.gathered, bf16[1024,3072]{1,0:T(8,128)(2,1)} %w_qkv.1, bf16[1024,1024]{1,0:T(8,128)(2,1)} %w_out.1, ...), custom_call_target="tpu_custom_call" | custom-call | flops 20000000000 | bytes 20000000 | tf_op jit(solution)/shard_map/pallas_call | solution.py:198
  (3 shorter events, 0.0 us)
Async XLA Ops:
  6.5 2.9 %copy-start = (bf16[384,1024]{1,0:T(8,128)(2,1)S(1)}, bf16[384,1024]{1,0:T(8,128)(2,1)}, u32[]{:S(2)}) copy-start(bf16[384,1024]{1,0:T(8,128)(2,1)} %frames.1) | copy-start | bytes 2359300
  6.5 2.9 %copy-start.1 = (f32[3,1024]{1,0:T(4,128)S(1)}, f32[3,1024]{1,0:T(4,128)}, u32[]{:S(2)}) copy-start(f32[3,1024]{1,0:T(4,128)} %modulation.1) | copy-start | bytes 36868
  6.5 105.7 %all-gather.2.cloned.1.call-start = ((), (), s32[]{:S(2)}) async-start(), calls=%async_computation | async-start | bytes 13369344 | tf_op jit(solution)/shard_map/all_gather | solution.py:225
Sparse Core Ops, SparseCore 0:
  10.9 101.3 all-gather.1
